TPU v7x, 32 devices: a whole 2x2x4 slice. The times are simulated.
32 devices in a mesh: dp: 16 (over z, x, core), mp: 2 (over y).
Axes of the slice: x: 2, y: 2, z: 4, core: 2. Of those that a mesh axis runs over, the one named last changes fastest.
Arguments:
- tokens: bfloat16 [6272, 512], P(('dp', 'mp')), may hold values from -6 to 6
- region_ids: int32 [32, 14, 14], P('dp'), may hold values from 0 to 3, as said below
- norm_gains: float32 [2, 2, 512], replicated, may hold values from 0.25 to 1.75
- norm_biases: float32 [2, 2, 512], replicated, may hold values from -2 to 2
- qkv_weight: bfloat16 [2, 512, 3, 512], P(None, 'dp', None, 'mp'), may hold values from -0.25 to 0.25
- qv_bias: float32 [2, 2, 512], P(None, None, 'mp'), may hold values from -3 to 3
- rel_table: float32 [2, 169, 16], P(None, None, 'mp'), may hold values from -4 to 4
- proj_weight: bfloat16 [2, 512, 512], P(None, 'mp', 'dp'), may hold values from -0.625 to 0.625
- proj_bias: float32 [2, 512], replicated, may hold values from -2 to 2
- fc1_weight: bfloat16 [2, 512, 2048], P(None, 'dp', 'mp'), may hold values from -0.25 to 0.25
- fc1_bias: float32 [2, 2048], P(None, 'mp'), may hold values from -3 to 3
- fc2_weight: bfloat16 [2, 2048, 512], P(None, 'mp', 'dp'), may hold values from -0.1875 to 0.1875
- fc2_bias: float32 [2, 512], replicated, may hold values from -2 to 2
- out_grad: bfloat16 [6272, 512], P(('dp', 'mp')), may hold values from -6 to 6
Outputs:
- block_out: bfloat16 [6272, 512], P(('dp', 'mp'))
- input_grad: bfloat16 [6272, 512], P(('dp', 'mp'))
- norm_gains_grad: float32 [2, 2, 512], replicated
- norm_biases_grad: float32 [2, 2, 512], replicated
- qkv_weight_grad: float32 [2, 512, 3, 512], P(None, 'dp', None, 'mp')
- qv_bias_grad: float32 [2, 2, 512], P(None, None, 'mp')
- rel_table_grad: float32 [2, 169, 16], P(None, None, 'mp')
- proj_weight_grad: float32 [2, 512, 512], P(None, 'mp', 'dp')
- proj_bias_grad: float32 [2, 512], replicated
- fc1_weight_grad: float32 [2, 512, 2048], P(None, 'dp', 'mp')
- fc1_bias_grad: float32 [2, 2048], P(None, 'mp')
- fc2_weight_grad: float32 [2, 2048, 512], P(None, 'mp', 'dp')
- fc2_bias_grad: float32 [2, 512], replicated
Inputs may be any that keep to these rules, and one draw needn't show every extreme that they name: `region_ids`: for each image, ids of four rectangular crops: id = 2 * [row >= cut_row] + [column >= cut_col] with cuts of 1 to 13 drawn per image, so every image holds all four ids.
All inputs are finite; a program needn't handle non-finite values.
Results may differ from a plain program's by a relative error of at most 0.02.
Values may be sent and summed in bfloat16 or wider, within the bound.
A program may use at most 128 MiB of HBM per device.

v0:
```python
import math

import jax
import jax.numpy as jnp
from jax import lax
from jax.sharding import PartitionSpec as P

HEAD_DIM = 32
GRID = 14
WINDOW = 7
SHIFT = 3
REL = 169


highest = lax.Precision.HIGHEST
masked_score = -100.0
epsilon = 1e-05
root_half = 1.0 / math.sqrt(2.0)
inverse_root = 1.0 / math.sqrt(2.0 * math.pi)
contract_rows = (((0,), (0,)), ((), ()))
contract_cols = (((1,), (1,)), ((), ()))


def layer_norm(values, gain_row, offset_row):
    centred = values - jnp.mean(values, axis=-1, keepdims=True)
    inverse = lax.rsqrt(jnp.mean(centred * centred, axis=-1, keepdims=True) + epsilon)
    normed = centred * inverse
    return (normed * gain_row + offset_row, normed, inverse)


def norm_back(gradient, normed, inverse, gain_row):
    scaled = gradient * gain_row
    inner = (
        scaled
        - jnp.mean(scaled, axis=-1, keepdims=True)
        - normed * jnp.mean(scaled * normed, axis=-1, keepdims=True)
    )
    return (inner * inverse, jnp.sum(gradient * normed, axis=0), jnp.sum(gradient, axis=0))


def slice_times(left_rows, weight_mat):
    return jnp.dot(left_rows, weight_mat, preferred_element_type=jnp.float32)


def slice_times_back(left_rows, weight_mat):
    return lax.dot_general(left_rows, weight_mat, contract_cols, preferred_element_type=jnp.float32)


def outer_sum(left_rows, right_rows):
    return lax.dot_general(left_rows, right_rows, contract_rows, preferred_element_type=jnp.float32)


def to_windows(rows, roll_by):
    images = rows.shape[0] // (GRID * GRID)
    width_all = rows.shape[1]
    grid_rows = rows.reshape(images, GRID, GRID, width_all)
    if roll_by:
        grid_rows = jnp.roll(grid_rows, (-roll_by, -roll_by), axis=(1, 2))
    blocks = GRID // WINDOW
    grid_rows = grid_rows.reshape(images, blocks, WINDOW, blocks, WINDOW, width_all).transpose(
        0, 1, 3, 2, 4, 5
    )
    return grid_rows.reshape(images * blocks * blocks, WINDOW * WINDOW, width_all)


def from_windows(windows, roll_by):
    blocks = GRID // WINDOW
    images = windows.shape[0] // (blocks * blocks)
    width_all = windows.shape[2]
    grid_rows = windows.reshape(images, blocks, blocks, WINDOW, WINDOW, width_all).transpose(
        0, 1, 3, 2, 4, 5
    )
    grid_rows = grid_rows.reshape(images, GRID, GRID, width_all)
    if roll_by:
        grid_rows = jnp.roll(grid_rows, (roll_by, roll_by), axis=(1, 2))
    return grid_rows.reshape(images * GRID * GRID, width_all)


def region_mask(region, roll_by):
    if roll_by:
        region = jnp.roll(region, (-roll_by, -roll_by), axis=(1, 2))
        places = jnp.arange(GRID, dtype=jnp.int32)
        band_id = (places >= GRID - WINDOW).astype(jnp.int32) + (places >= GRID - roll_by).astype(
            jnp.int32
        )
        region = region * 9 + band_id[None, :, None] * 3 + band_id[None, None, :]
    labels = to_windows(region.reshape(-1, 1), 0)[:, :, 0]
    return jnp.where(labels[:, :, None] == labels[:, None, :], 0.0, masked_score).astype(
        jnp.float32
    )


def position_index():
    places = jnp.arange(WINDOW * WINDOW, dtype=jnp.int32)
    row_of = places // WINDOW
    col_of = places % WINDOW
    return (row_of[:, None] - row_of[None, :] + WINDOW - 1) * (2 * WINDOW - 1) + (
        col_of[:, None] - col_of[None, :] + WINDOW - 1
    )


def window_scores(windows, relative, score_mask):
    scores = jnp.einsum(
        "wqhd,wkhd->whqk", windows[:, :, 0], windows[:, :, 1], preferred_element_type=jnp.float32
    )
    return scores * HEAD_DIM ** (-0.5) + relative[None] + score_mask[:, None]


def per_device(
    tokens,
    region_ids,
    norm_gains,
    norm_biases,
    qkv_weight,
    qv_bias,
    rel_table,
    proj_weight,
    proj_bias,
    fc1_weight,
    fc1_bias,
    fc2_weight,
    fc2_bias,
    out_grad,
):
    layer_total = qkv_weight.shape[0]
    width_all = tokens.shape[1]
    local_width = qkv_weight.shape[3]
    head_local = rel_table.shape[2]
    hidden_local = fc1_weight.shape[2]
    pair_index = position_index().reshape(-1)
    one_hot = (pair_index[:, None] == jnp.arange(REL, dtype=jnp.int32)[None, :]).astype(jnp.float32)
    masks_all = (region_mask(region_ids, 0), region_mask(region_ids, SHIFT))
    state = tokens.astype(jnp.float32)
    records = []
    for depth in range(layer_total):
        roll_by = SHIFT if depth % 2 == 1 else 0
        weights = (
            lax.all_gather(qkv_weight[depth], "dp", axis=0, tiled=True),
            lax.all_gather(proj_weight[depth], "dp", axis=1, tiled=True),
            lax.all_gather(fc1_weight[depth], "dp", axis=0, tiled=True),
            lax.all_gather(fc2_weight[depth], "dp", axis=1, tiled=True),
        )
        normed_one, hat_one, inverse_one = layer_norm(
            state, norm_gains[depth, 0], norm_biases[depth, 0]
        )
        rows_one = lax.all_gather(normed_one.astype(jnp.bfloat16), "mp", axis=0, tiled=True)
        packed = jnp.dot(
            rows_one,
            weights[0].reshape(width_all, 3 * local_width),
            preferred_element_type=jnp.float32,
        )
        bias_rows = jnp.concatenate(
            [qv_bias[depth, 0], jnp.zeros_like(qv_bias[depth, 0]), qv_bias[depth, 1]]
        )
        packed = (packed + bias_rows).astype(jnp.bfloat16)
        windows = to_windows(packed, roll_by).reshape(-1, WINDOW * WINDOW, 3, head_local, HEAD_DIM)
        relative = (
            jnp.dot(one_hot, rel_table[depth], precision=highest)
            .reshape(WINDOW * WINDOW, WINDOW * WINDOW, head_local)
            .transpose(2, 0, 1)
        )
        scores = window_scores(windows, relative, masks_all[depth % 2])
        highest_score = jnp.max(scores, axis=-1, keepdims=True)
        raised = jnp.exp(scores - highest_score)
        sums_row = jnp.sum(raised, axis=-1, keepdims=True)
        chances = (raised / sums_row).astype(jnp.bfloat16)
        log_total = highest_score + jnp.log(sums_row)
        mixed = jnp.einsum(
            "whqk,wkhd->wqhd", chances, windows[:, :, 2], preferred_element_type=jnp.float32
        ).astype(jnp.bfloat16)
        merged = from_windows(mixed.reshape(-1, WINDOW * WINDOW, local_width), roll_by)
        attn_sum = lax.psum_scatter(
            slice_times(merged, weights[1]).astype(jnp.bfloat16),
            "mp",
            scatter_dimension=0,
            tiled=True,
        ).astype(jnp.float32)
        middle = state + (attn_sum + proj_bias[depth])
        normed_two, hat_two, inverse_two = layer_norm(
            middle, norm_gains[depth, 1], norm_biases[depth, 1]
        )
        rows_two = lax.all_gather(normed_two.astype(jnp.bfloat16), "mp", axis=0, tiled=True)
        pre_act = (
            jnp.dot(rows_two, weights[2], preferred_element_type=jnp.float32) + fc1_bias[depth]
        )
        active = jax.nn.gelu(pre_act, approximate=False).astype(jnp.bfloat16)
        mlp_sum = lax.psum_scatter(
            slice_times(active, weights[3]).astype(jnp.bfloat16),
            "mp",
            scatter_dimension=0,
            tiled=True,
        ).astype(jnp.float32)
        state = middle + (mlp_sum + fc2_bias[depth])
        records.append(
            (
                weights,
                hat_one,
                inverse_one,
                rows_one,
                windows,
                log_total,
                merged,
                hat_two,
                inverse_two,
                rows_two,
                pre_act,
                active,
            )
        )
    block_out = state.astype(jnp.bfloat16)
    gradient = out_grad.astype(jnp.float32)
    grads_weight = []
    small_rows = []
    for depth in reversed(range(layer_total)):
        roll_by = SHIFT if depth % 2 == 1 else 0
        (
            saved_weights,
            hat_one,
            inverse_one,
            rows_one,
            windows,
            log_total,
            merged,
            hat_two,
            inverse_two,
            rows_two,
            pre_act,
            active,
        ) = records[depth]
        weights = (
            lax.all_gather(qkv_weight[depth], "dp", axis=0, tiled=True),
            lax.all_gather(proj_weight[depth], "dp", axis=1, tiled=True),
            lax.all_gather(fc1_weight[depth], "dp", axis=0, tiled=True),
            lax.all_gather(fc2_weight[depth], "dp", axis=1, tiled=True),
        )
        mlp_grad = gradient.astype(jnp.bfloat16)
        down_bias_sum = jnp.sum(mlp_grad.astype(jnp.float32), axis=0)
        mlp_grad_rows = lax.all_gather(mlp_grad, "mp", axis=0, tiled=True)
        down_sum = outer_sum(active, mlp_grad_rows)
        active_grad = lax.dot_general(
            mlp_grad_rows, weights[3], contract_cols, preferred_element_type=jnp.float32
        )
        slope = (
            0.5 * (1.0 + lax.erf(pre_act * root_half))
            + pre_act * jnp.exp(-0.5 * pre_act * pre_act) * inverse_root
        )
        pre_grad = (active_grad * slope).astype(jnp.bfloat16)
        up_bias_sum = jnp.sum(pre_grad.astype(jnp.float32), axis=0)
        up_sum = outer_sum(rows_two, pre_grad)
        norm_two_grad = lax.psum_scatter(
            slice_times_back(pre_grad, weights[2]).astype(jnp.bfloat16),
            "mp",
            scatter_dimension=0,
            tiled=True,
        ).astype(jnp.float32)
        back_two, gain_two_grad, offset_two_grad = norm_back(
            norm_two_grad, hat_two, inverse_two, norm_gains[depth, 1]
        )
        gradient = gradient + back_two
        attn_grad = gradient.astype(jnp.bfloat16)
        proj_bias_sum = jnp.sum(attn_grad.astype(jnp.float32), axis=0)
        attn_grad_rows = lax.all_gather(attn_grad, "mp", axis=0, tiled=True)
        proj_sum = outer_sum(merged, attn_grad_rows)
        mixed_grad = lax.dot_general(
            attn_grad_rows, weights[1], contract_cols, preferred_element_type=jnp.float32
        ).astype(jnp.bfloat16)
        mixed_grad = to_windows(mixed_grad, roll_by).reshape(
            -1, WINDOW * WINDOW, head_local, HEAD_DIM
        )
        relative = (
            jnp.dot(one_hot, rel_table[depth], precision=highest)
            .reshape(WINDOW * WINDOW, WINDOW * WINDOW, head_local)
            .transpose(2, 0, 1)
        )
        scores = window_scores(windows, relative, masks_all[depth % 2])
        chances_full = jnp.exp(scores - log_total)
        chances = chances_full.astype(jnp.bfloat16)
        value_grad = jnp.einsum(
            "whqk,wqhd->wkhd", chances, mixed_grad, preferred_element_type=jnp.float32
        )
        chance_grad = jnp.einsum(
            "wqhd,wkhd->whqk", mixed_grad, windows[:, :, 2], preferred_element_type=jnp.float32
        )
        score_grad = (
            chances_full
            * (chance_grad - jnp.sum(chance_grad * chances_full, axis=-1, keepdims=True))
        ).astype(jnp.bfloat16)
        pair_sums = jnp.sum(score_grad.astype(jnp.float32), axis=0).reshape(head_local, -1)
        table_sum = lax.dot_general(one_hot, pair_sums, (((0,), (1,)), ((), ())), precision=highest)
        scaling = HEAD_DIM ** (-0.5)
        query_grad = (
            jnp.einsum(
                "whqk,wkhd->wqhd", score_grad, windows[:, :, 1], preferred_element_type=jnp.float32
            )
            * scaling
        )
        key_grad = (
            jnp.einsum(
                "whqk,wqhd->wkhd", score_grad, windows[:, :, 0], preferred_element_type=jnp.float32
            )
            * scaling
        )
        stacked = jnp.stack([query_grad, key_grad, value_grad], axis=2).reshape(
            -1, WINDOW * WINDOW, 3 * local_width
        )
        packed_grad = from_windows(stacked, roll_by).astype(jnp.bfloat16)
        column_sums = jnp.sum(packed_grad.astype(jnp.float32), axis=0).reshape(3, local_width)
        qv_sum = jnp.stack([column_sums[0], column_sums[2]])
        qkv_sum = outer_sum(rows_one, packed_grad).reshape(width_all, 3, local_width)
        norm_one_grad = lax.psum_scatter(
            slice_times_back(packed_grad, weights[0].reshape(width_all, 3 * local_width)).astype(
                jnp.bfloat16
            ),
            "mp",
            scatter_dimension=0,
            tiled=True,
        ).astype(jnp.float32)
        back_one, gain_one_grad, offset_one_grad = norm_back(
            norm_one_grad, hat_one, inverse_one, norm_gains[depth, 0]
        )
        gradient = gradient + back_one
        shards = (
            lax.psum_scatter(qkv_sum, "dp", scatter_dimension=0, tiled=True),
            lax.psum_scatter(proj_sum, "dp", scatter_dimension=1, tiled=True),
            lax.psum_scatter(up_sum, "dp", scatter_dimension=0, tiled=True),
            lax.psum_scatter(down_sum, "dp", scatter_dimension=1, tiled=True),
        )
        grads_weight.append(shards)
        small_rows.append(
            (
                jnp.stack([gain_one_grad, gain_two_grad]),
                jnp.stack([offset_one_grad, offset_two_grad]),
                qv_sum,
                table_sum,
                proj_bias_sum,
                up_bias_sum,
                down_bias_sum,
            )
        )
    grads_weight = grads_weight[::-1]
    small_rows = small_rows[::-1]

    def stack_weight(position):
        return jnp.stack([entry[position] for entry in grads_weight])

    weight_totals = (stack_weight(0), stack_weight(1), stack_weight(2), stack_weight(3))
    mp_count = lax.axis_size("mp")
    mp_index = lax.axis_index("mp")

    def stack_member(position):
        return jnp.stack([entry[position] for entry in small_rows])

    qv_full = lax.dynamic_update_slice(
        jnp.zeros((layer_total, 2, local_width * mp_count), jnp.float32),
        stack_member(2),
        (0, 0, mp_index * local_width),
    )
    table_full = lax.dynamic_update_slice(
        jnp.zeros((layer_total, REL, head_local * mp_count), jnp.float32),
        stack_member(3),
        (0, 0, mp_index * head_local),
    )
    up_full = lax.dynamic_update_slice(
        jnp.zeros((layer_total, hidden_local * mp_count), jnp.float32),
        stack_member(5),
        (0, mp_index * hidden_local),
    )
    totals = lax.psum(
        (
            stack_member(0),
            stack_member(1),
            qv_full,
            table_full,
            stack_member(4),
            up_full,
            stack_member(6),
        ),
        ("dp", "mp"),
    )
    return (
        block_out,
        gradient.astype(jnp.bfloat16),
        totals[0],
        totals[1],
        weight_totals[0],
        lax.dynamic_slice_in_dim(totals[2], mp_index * local_width, local_width, 2),
        lax.dynamic_slice_in_dim(totals[3], mp_index * head_local, head_local, 2),
        weight_totals[1],
        totals[4],
        weight_totals[2],
        lax.dynamic_slice_in_dim(totals[5], mp_index * hidden_local, hidden_local, 1),
        weight_totals[3],
        totals[6],
    )


def solution(mesh):
    in_specs = (
        P(("dp", "mp"), None),
        P("dp", None, None),
        P(),
        P(),
        P(None, "dp", None, "mp"),
        P(None, None, "mp"),
        P(None, None, "mp"),
        P(None, "mp", "dp"),
        P(),
        P(None, "dp", "mp"),
        P(None, "mp"),
        P(None, "mp", "dp"),
        P(),
        P(("dp", "mp"), None),
    )
    out_specs = (
        P(("dp", "mp"), None),
        P(("dp", "mp"), None),
        P(),
        P(),
        P(None, "dp", None, "mp"),
        P(None, None, "mp"),
        P(None, None, "mp"),
        P(None, "mp", "dp"),
        P(),
        P(None, "dp", "mp"),
        P(None, "mp"),
        P(None, "mp", "dp"),
        P(),
    )
    return jax.shard_map(
        per_device, mesh=mesh, in_specs=in_specs, out_specs=out_specs, check_vma=False
    )
```

profile of v0, /device:TPU:0, one launch (start us, length us, event | category | flops | bytes accessed | tf_op | source)
XLA Modules:
  0.0 1124.8 jit_solution(17824669784708326473)
XLA Ops:
  19.4 8.7 all-gather.8
  29.0 25.3 %all-gather = bf16[1,512,3,256]{3,1,2,0:T(8,128)(2,1)S(1)} all-gather(bf16[1,32,3,256]{3,1,2,0:T(8,128)(2,1)S(1)} %get-tuple-element.68), channel_id=2, replica_groups=mesh['dp'=16,'mp'=2] {'dp'}, dimensions={1}, use_global_device_ids=true | all-gather | bytes 835584 | tf_op jit(solution)/shard_map/all_gather | solution.py:138
  77.9 18.8 %all-gather.1 = bf16[1,256,512]{1,2,0:T(8,128)(2,1)S(1)} all-gather(bf16[1,256,32]{1,2,0:T(8,128)(2,1)S(1)} %get-tuple-element.70), channel_id=3, replica_groups=mesh['dp'=16,'mp'=2] {'dp'}, dimensions={2}, use_global_device_ids=true | all-gather | bytes 278528 | tf_op jit(solution)/shard_map/all_gather | solution.py:139
  97.0 10.1 fusion
  116.7 21.8 %all-gather.4 = bf16[1,512,3,256]{3,1,2,0:T(8,128)(2,1)S(1)} all-gather(bf16[1,32,3,256]{3,1,2,0:T(8,128)(2,1)S(1)} %copy-done.48), channel_id=6, replica_groups=mesh['dp'=16,'mp'=2] {'dp'}, dimensions={1}, use_global_device_ids=true | all-gather | bytes 835584 | tf_op jit(solution)/shard_map/all_gather | solution.py:138
  138.5 18.5 %all-gather.5 = bf16[1,256,512]{1,2,0:T(8,128)(2,1)S(1)} all-gather(bf16[1,256,32]{1,2,0:T(8,128)(2,1)S(1)} %get-tuple-element.69), channel_id=7, replica_groups=mesh['dp'=16,'mp'=2] {'dp'}, dimensions={2}, use_global_device_ids=true | all-gather | bytes 278528 | tf_op jit(solution)/shard_map/all_gather | solution.py:139
  162.0 8.1 all-gather.9
  171.9 6.4 fusion.19
  181.3 9.7 fusion.1
  195.1 6.9 all-gather.12
  210.0 7.2 all-gather.10
  259.2 10.2 fusion.2
  277.2 7.2 all-gather.11
  286.2 6.4 fusion.22
  298.5 10.8 fusion.4
  322.9 6.7 all-gather.13
  350.7 5.9 copy.110
  376.4 9.1 fusion.5
  400.3 7.4 all-gather.14
  414.4 8.8 fusion.6
  438.0 6.5 all-gather.15
  459.3 5.3 copy.119
  471.8 10.8 fusion.167
  518.9 92.8 %all-reduce.20.cloned.1.call-done = (f32[2,2,512]{2,1,0:T(2,128)}, f32[2,2,512]{2,1,0:T(2,128)}, f32[2,2,512]{2,1,0:T(2,128)}, f32[2,169,16]{1,2,0:T(8,128)}, f3...) async-done(((f32[2,2,512]{2,1,0:T(2,128)}, f32[2,2,512]{2,1,0:T(2,128)}, f32[2,2,512]{2,1,0:T(2,128)}, f32[2,169,16]{1,2,0:T(8,128)}, f32[2,512]{1,0:T(2,128)}, ...) | async-done | bytes 70800 | tf_op jit(solution)/shard_map/psum | solution.py:368
  615.7 56.9 %reduce-scatter.31.cloned.1.call-done = f32[256,32]{0,1:T(8,128)} async-done(((f32[256,512]{0,1:T(8,128)}), f32[256,32]{0,1:T(8,128)}) %reduce-scatter.31.cloned.1.call-update) | async-done | bytes 32784 | tf_op jit(solution)/shard_map/reduce_scatter | solution.py:324
  672.6 58.4 %reduce-scatter.29.cloned.1.call-done = f32[256,32]{0,1:T(8,128)} async-done(((f32[256,512]{0,1:T(8,128)}), f32[256,32]{0,1:T(8,128)}) %reduce-scatter.29.cloned.1.call-update) | async-done | bytes 32784 | tf_op jit(solution)/shard_map/reduce_scatter | solution.py:324
  732.4 61.3 %reduce-scatter.27.cloned.1.call-done = f32[32,3,256]{2,0,1:T(8,128)} async-done(((f32[512,3,256]{2,0,1:T(8,128)}), f32[32,3,256]{2,0,1:T(8,128)}) %reduce-scatter.27.cloned.1.call-update) | async-done | bytes 98320 | tf_op jit(solution)/shard_map/reduce_scatter | solution.py:323
  793.6 62.1 %reduce-scatter.25.cloned.1.call-done = f32[32,3,256]{2,0,1:T(8,128)} async-done(((f32[512,3,256]{2,0,1:T(8,128)}), f32[32,3,256]{2,0,1:T(8,128)}) %reduce-scatter.25.cloned.1.call-update) | async-done | bytes 98320 | tf_op jit(solution)/shard_map/reduce_scatter | solution.py:323
  857.4 63.0 %reduce-scatter.39.cloned.1.call-done = f32[1024,32]{0,1:T(8,128)} async-done(((f32[1024,512]{0,1:T(8,128)}), f32[1024,32]{0,1:T(8,128)}) %reduce-scatter.39.cloned.1.call-update) | async-done | bytes 131088 | tf_op jit(solution)/shard_map/reduce_scatter | solution.py:326
  920.4 64.4 %reduce-scatter.37.cloned.1.call-done = f32[1024,32]{0,1:T(8,128)} async-done(((f32[1024,512]{0,1:T(8,128)}), f32[1024,32]{0,1:T(8,128)}) %reduce-scatter.37.cloned.1.call-update) | async-done | bytes 131088 | tf_op jit(solution)/shard_map/reduce_scatter | solution.py:326
  986.4 63.0 %reduce-scatter.35.cloned.1.call-done = f32[32,1024]{1,0:T(8,128)} async-done(((f32[512,1024]{1,0:T(8,128)}), f32[32,1024]{1,0:T(8,128)}) %reduce-scatter.35.cloned.1.call-update) | async-done | bytes 131088 | tf_op jit(solution)/shard_map/reduce_scatter | solution.py:325
  1049.4 64.4 %reduce-scatter.33.cloned.1.call-done = f32[32,1024]{1,0:T(8,128)} async-done(((f32[512,1024]{1,0:T(8,128)}), f32[32,1024]{1,0:T(8,128)}) %reduce-scatter.33.cloned.1.call-update) | async-done | bytes 131088 | tf_op jit(solution)/shard_map/reduce_scatter | solution.py:325
  (476 shorter events, 285.6 us)
Async XLA Ops:
  7.2 164.7 %all-gather.21.cloned.1.call-start = ((), (), s32[]{:S(2)}) async-start(), calls=%async_computation.16 | async-start | bytes 1114112 | tf_op jit(solution)/shard_map/all_gather | solution.py:140
  8.8 169.6 %all-gather.23.cloned.1.call-start = ((), (), s32[]{:S(2)}) async-start(), calls=%async_computation.17 | async-start | bytes 1114112 | tf_op jit(solution)/shard_map/all_gather | solution.py:141
  10.4 275.8 %all-gather.25.cloned.1.call-start = ((), (), s32[]{:S(2)}) async-start(), calls=%async_computation.18 | async-start | bytes 1114112 | tf_op jit(solution)/shard_map/all_gather | solution.py:140
  11.2 281.4 %all-gather.27.cloned.1.call-start = ((), (), s32[]{:S(2)}) async-start(), calls=%async_computation.19 | async-start | bytes 1114112 | tf_op jit(solution)/shard_map/all_gather | solution.py:141
  77.7 36.6 %copy-start.89 = (f32[2,512]{1,0:T(2,128)S(1)}, f32[2,512]{1,0:T(2,128)}, u32[]{:S(2)}) copy-start(f32[2,512]{1,0:T(2,128)} %param.26) | copy-start | bytes 12292
  77.7 37.2 %copy-start.84 = (f32[2,1024]{1,0:T(2,128)S(1)}, f32[2,1024]{1,0:T(2,128)}, u32[]{:S(2)}) copy-start(f32[2,1024]{1,0:T(2,128)} %param.24) | copy-start | bytes 24580
  77.8 38.9 %copy-start.30 = (bf16[392,256]{1,0:T(8,128)(2,1)}, bf16[392,256]{1,0:T(8,128)(2,1)S(1)}, u32[]{:S(2)}) copy-start(bf16[392,256]{1,0:T(8,128)(2,1)S(1)} %reshape_reshape.35) | copy-start | bytes 602116
  77.9 38.8 %copy-start.48 = (bf16[1,32,3,256]{3,1,2,0:T(8,128)(2,1)S(1)}, bf16[1,32,3,256]{3,1,2,0:T(8,128)(2,1)}, u32[]{:S(2)}) copy-start(bf16[1,32,3,256]{3,1,2,0:T(8,128)(2,1)} %get-tuple-element.67) | copy-start | bytes 147460
  96.7 41.9 %copy-start.23 = (bf16[1,256,512]{1,2,0:T(8,128)(2,1)}, bf16[1,256,512]{1,2,0:T(8,128)(2,1)S(1)}, u32[]{:S(2)}) copy-start(bf16[1,256,512]{1,2,0:T(8,128)(2,1)S(1)} %all-gather.1) | copy-start | bytes 786436
  107.8 51.2 %collective-permute-start = (bf16[4,512]{1,0:T(4,128)(2,1)}, bf16[4,512]{1,0:T(4,128)(2,1)}, u32[]{:S(2)}, u32[]{:S(2)}) collective-permute-start(bf16[4,512]{1,0:T(4,128)(2,1)} %slice.312), channel_id=1, source_target_pairs={{0,1},{2,3},{4,5},{6,7},{8,9},{10,11},{12,13},{14,15},{16,17},{18,... | collective-permute-start | bytes 12296
  110.9 500.9 %all-reduce.20.cloned.1.call-start = ((), (), s32[]{:S(2)}) async-start(), calls=%async_computation.20 | async-start | bytes 163840 | tf_op jit(solution)/shard_map/psum | solution.py:368
  113.7 47.4 %copy-start.52 = (f32[1,1,512]{2,1,0:T(1,128)S(1)}, f32[1,1,512]{2,1,0:T(1,128)}, u32[]{:S(2)}) copy-start(f32[1,1,512]{2,1,0:T(1,128)} %get-tuple-element.74) | copy-start | bytes 6148
  157.0 100.1 %copy-start.24 = (bf16[1,256,512]{1,2,0:T(8,128)(2,1)}, bf16[1,256,512]{1,2,0:T(8,128)(2,1)S(1)}, u32[]{:S(2)}) copy-start(bf16[1,256,512]{1,2,0:T(8,128)(2,1)S(1)} %all-gather.5) | copy-start | bytes 786436
  191.7 15.9 %collective-permute-start.1 = (bf16[4,512]{1,0:T(4,128)(2,1)S(1)}, bf16[4,512]{1,0:T(4,128)(2,1)S(1)}, u32[]{:S(2)}, u32[]{:S(2)}) collective-permute-start(bf16[4,512]{1,0:T(4,128)(2,1)S(1)} %slice.313), channel_id=1, source_target_pairs={{0,1},{2,3},{4,5},{6,7},{8,9},{10,11},{12,13},{14,15},{16,17},{18,... | collective-permute-start | bytes 12296
  269.4 3.3 collective-permute-start.2
  310.0 5.3 collective-permute-start.4
  386.1 7.3 collective-permute-start.5
  423.9 6.6 collective-permute-start.6
  482.6 4.4 collective-permute-start.7
  488.9 183.7 %reduce-scatter.31.cloned.1.call-start = ((), (), s32[]{:S(2)}) async-start(), calls=%async_computation.11 | async-start | bytes 557056 | tf_op jit(solution)/shard_map/reduce_scatter | solution.py:324
  490.2 240.8 %reduce-scatter.29.cloned.1.call-start = ((), (), s32[]{:S(2)}) async-start(), calls=%async_computation.10 | async-start | bytes 557056 | tf_op jit(solution)/shard_map/reduce_scatter | solution.py:324
  491.5 302.2 %reduce-scatter.27.cloned.1.call-start = ((), (), s32[]{:S(2)}) async-start(), calls=%async_computation.9 | async-start | bytes 1671168 | tf_op jit(solution)/shard_map/reduce_scatter | solution.py:323
  495.2 360.5 %reduce-scatter.25.cloned.1.call-start = ((), (), s32[]{:S(2)}) async-start(), calls=%async_computation.8 | async-start | bytes 1671168 | tf_op jit(solution)/shard_map/reduce_scatter | solution.py:323
  497.2 423.2 %reduce-scatter.39.cloned.1.call-start = ((), (), s32[]{:S(2)}) async-start(), calls=%async_computation.15 | async-start | bytes 2228224 | tf_op jit(solution)/shard_map/reduce_scatter | solution.py:326
  500.4 484.3 %reduce-scatter.37.cloned.1.call-start = ((), (), s32[]{:S(2)}) async-start(), calls=%async_computation.14 | async-start | bytes 2228224 | tf_op jit(solution)/shard_map/reduce_scatter | solution.py:326
  503.8 545.6 %reduce-scatter.35.cloned.1.call-start = ((), (), s32[]{:S(2)}) async-start(), calls=%async_computation.13 | async-start | bytes 2228224 | tf_op jit(solution)/shard_map/reduce_scatter | solution.py:325
  507.2 606.6 %reduce-scatter.33.cloned.1.call-start = ((), (), s32[]{:S(2)}) async-start(), calls=%async_computation.12 | async-start | bytes 2228224 | tf_op jit(solution)/shard_map/reduce_scatter | solution.py:325
  511.4 5.5 collective-permute-start.3
  611.8 503.7 %copy-start.86 = (f32[2,2,512]{2,1,0:T(2,128)S(1)}, f32[2,2,512]{2,1,0:T(2,128)}, u32[]{:S(2)}) copy-start(f32[2,2,512]{2,1,0:T(2,128)} %get-tuple-element.117) | copy-start | bytes 24580
  611.8 504.3 %copy-start.85 = (f32[2,2,512]{2,1,0:T(2,128)S(1)}, f32[2,2,512]{2,1,0:T(2,128)}, u32[]{:S(2)}) copy-start(f32[2,2,512]{2,1,0:T(2,128)} %get-tuple-element.118) | copy-start | bytes 24580
  611.8 504.9 %copy-start.92 = (f32[2,512]{1,0:T(2,128)S(1)}, f32[2,512]{1,0:T(2,128)}, u32[]{:S(2)}) copy-start(f32[2,512]{1,0:T(2,128)} %get-tuple-element.123) | copy-start | bytes 12292
  611.8 505.5 %copy-start.91 = (f32[2,512]{1,0:T(2,128)S(1)}, f32[2,512]{1,0:T(2,128)}, u32[]{:S(2)}) copy-start(f32[2,512]{1,0:T(2,128)} %get-tuple-element.127) | copy-start | bytes 12292
  (87 other events, 702.1 us)
Sparse Core Ops, SparseCore 0:
  10.8 43.3 all-gather.20
  56.3 37.3 all-gather.22
  96.5 37.8 all-gather.24
  136.4 38.3 all-gather.26
  489.1 122.6 all-reduce.19
  615.6 56.9 reduce-scatter.30
  676.2 54.7 reduce-scatter.28
  735.1 58.5 reduce-scatter.26
  797.3 58.4 reduce-scatter.24
  859.8 60.5 reduce-scatter.38
  924.1 60.5 reduce-scatter.36
  988.8 60.5 reduce-scatter.34
  1053.1 60.5 reduce-scatter.32
where the time goes:
time: 1140 us; the launch traced here: 1120 us
  waiting for transfers between devices  590 us (52%)
  blocking collectives  213 us (19%)
  local copies, waits for them, and re-layouts  156 us (14%)
  matrix products  78.3 us (7%)
  other arithmetic  44.2 us (4%)
  starting transfers between devices  26.9 us (2%)
  between operations  16.3 us (1%)
    reduce_scatter x2, waiting for transfers between devices, per_device(): lax.psum_scatter(down_sum, 'dp', scatter_dimension=1, tiled=True)  127 us
    reduce_scatter x2, waiting for transfers between devices, per_device(): lax.psum_scatter(up_sum, 'dp', scatter_dimension=0, tiled=True)  127 us
    reduce_scatter x2, waiting for transfers between devices, per_device(): lax.psum_scatter(qkv_sum, 'dp', scatter_dimension=0, tiled=True)  123 us
    reduce_scatter x2, waiting for transfers between devices, per_device(): lax.psum_scatter(proj_sum, 'dp', scatter_dimension=1, tiled=True)  115 us
    psum x1, waiting for transfers between devices, per_device(): lax.psum((stack_member(0), stack_member(1), qv_full, table_full, stack_me...  92.8 us
    unnamed x7, blocking collectives  69.5 us
    unnamed x233, local copies, waits for them, and re-layouts  58.6 us
    all_gather x2, blocking collectives, per_device(): lax.all_gather(qkv_weight[depth], 'dp', axis=0, tiled=True)  47.1 us
  transfers between devices with their start and end apart: 21, of which 12 were waited for; matrix products, arithmetic and copies ran while one was open for 16% of the time, Pallas kernels for 0%

commit v1 on v0

v1 whole, which is shorter than its diff:
```python
import functools
import math

import jax
import jax.numpy as jnp
import numpy as np
from jax import lax
from jax.experimental import pallas as pl
from jax.experimental.pallas import tpu as pltpu
from jax.sharding import PartitionSpec as P

HEAD_DIM = 32
GRID = 14
WINDOW = 7
SHIFT = 3
REL = 169
AREA = WINDOW * WINDOW
SLOT = 64
ROWS = 256
WIDTH = 512
QKV = 768
HALF = 256
HID = 1024
COLS = QKV + HALF + HID + HID
HEADS = 16

masked_score = -100.0
blocked = -1e30
epsilon = 1e-05
root_half = 1.0 / math.sqrt(2.0)
inverse_root = 1.0 / math.sqrt(2.0 * math.pi)
scaling = HEAD_DIM ** (-0.5)
f32 = jnp.float32
bf16 = jnp.bfloat16


def dot_nn(a, b):
    return lax.dot_general(a, b, (((1,), (0,)), ((), ())), preferred_element_type=f32)


def dot_nt(a, b):
    return lax.dot_general(a, b, (((1,), (1,)), ((), ())), preferred_element_type=f32)


def dot_tn(a, b):
    return lax.dot_general(a, b, (((0,), (0,)), ((), ())), preferred_element_type=f32)


def token_places(roll_by):
    places = np.full((ROWS,), -1, np.int32)
    for window in range(4):
        for at in range(AREA):
            row = (window // 2) * WINDOW + at // WINDOW
            col = (window % 2) * WINDOW + at % WINDOW
            places[window * SLOT + at] = ((row + roll_by) % GRID) * GRID + (col + roll_by) % GRID
    return places


def permutation(roll_by):
    return (token_places(roll_by)[:, None] == np.arange(ROWS)[None, :]).astype(np.float32)


def permute(dot, perm, values):
    high = values.astype(bf16)
    rest = values - high.astype(f32)
    mid = rest.astype(bf16)
    low = (rest - mid.astype(f32)).astype(bf16)
    return (dot(perm, high) + dot(perm, mid)) + dot(perm, low)


def normalise(values):
    centred = values - jnp.mean(values, axis=-1, keepdims=True)
    inverse = lax.rsqrt(jnp.mean(centred * centred, axis=-1, keepdims=True) + epsilon)
    return centred * inverse, inverse


def norm_back(gradient, normed, inverse, gain_row):
    scaled = gradient * gain_row
    inner = (
        scaled
        - jnp.mean(scaled, axis=-1, keepdims=True)
        - normed * jnp.mean(scaled * normed, axis=-1, keepdims=True)
    )
    return (
        inner * inverse,
        jnp.sum(gradient * normed, axis=0, keepdims=True),
        jnp.sum(gradient, axis=0, keepdims=True),
    )


def weight(ref, half, start, width):
    return ref[:, half, :, start : start + width].reshape(WIDTH, width)


def lane_mask(head):
    lane = lax.broadcasted_iota(jnp.int32, (1, 128), 1)
    return jnp.where(lane // HEAD_DIM == head, 1.0, 0.0).astype(bf16)


def head_probs(query, key, rel_half, mask):
    relative = jnp.concatenate([rel_half, rel_half], axis=0)
    scores = dot_nt(query, key) * scaling + relative + mask
    raised = jnp.exp(scores - jnp.max(scores, axis=-1, keepdims=True))
    return raised / jnp.sum(raised, axis=-1, keepdims=True)


def forward_kernel(
    x_ref, perm_ref, w_ref, gain_ref, off_ref, qkvb_ref, rel_ref, mask_ref, projb_ref, upb_ref,
    downb_ref, out_ref, xw_ref, mid_ref, qkv_ref, mixed_ref, slope_ref, act_ref,
):
    perm = perm_ref[...]
    xw = permute(dot_nn, perm, x_ref[...])
    xw_ref[...] = xw
    normed = (normalise(xw)[0] * gain_ref[0:1, :] + off_ref[0:1, :]).astype(bf16)
    for m in range(2):
        packed = dot_nn(normed, weight(w_ref, m, 0, QKV)) + qkvb_ref[m : m + 1, :]
        qkv_ref[m] = packed.astype(bf16)

    def group(i, carry):
        m = i // 2
        lanes = pl.multiple_of((i % 2) * 128, 128)
        for p in range(2):
            rows = slice(p * 128, p * 128 + 128)
            query = qkv_ref[m, rows, pl.ds(lanes, 128)]
            key = qkv_ref[m, rows, pl.ds(lanes + HALF, 128)]
            value = qkv_ref[m, rows, pl.ds(lanes + 2 * HALF, 128)]
            total = jnp.zeros((128, 128), f32)
            for h in range(4):
                sel = lane_mask(h)
                probs = head_probs(query * sel, key, rel_ref[i * 4 + h], mask_ref[p])
                total = total + dot_nn(probs.astype(bf16), value * sel)
            mixed_ref[m, rows, pl.ds(lanes, 128)] = total.astype(bf16)
        return carry

    lax.fori_loop(0, 4, group, 0)
    mid = xw + (
        dot_nt(mixed_ref[0], weight(w_ref, 0, QKV, HALF))
        + dot_nt(mixed_ref[1], weight(w_ref, 1, QKV, HALF))
        + projb_ref[...]
    )
    mid_ref[...] = mid
    normed = (normalise(mid)[0] * gain_ref[1:2, :] + off_ref[1:2, :]).astype(bf16)
    branch = jnp.zeros((ROWS, WIDTH), f32)
    for m in range(2):
        pre = dot_nn(normed, weight(w_ref, m, QKV + HALF, HID)) + upb_ref[m : m + 1, :]
        cdf = 0.5 * (1.0 + lax.erf(pre * root_half))
        active = (pre * cdf).astype(bf16)
        slope_ref[m] = cdf + pre * jnp.exp(-0.5 * pre * pre) * inverse_root
        act_ref[m] = active
        branch = branch + dot_nt(active, weight(w_ref, m, QKV + HALF + HID, HID))
    out_ref[...] = permute(dot_tn, perm, mid + (branch + downb_ref[...]))


def backward_kernel(
    g_ref, perm_ref, w_ref, gain_ref, off_ref, rel_ref, mask_ref, xw_ref, mid_ref, qkv_ref,
    mixed_ref, slope_ref, act_ref,
    out_ref, wg_ref, gaing_ref, offg_ref, qkvbg_ref, projbg_ref, upbg_ref, downbg_ref, relg_ref,
    dmix_ref, dqkv_ref,
):
    def put(m, start, width, value):
        wg_ref[:, m, :, start : start + width] = value.astype(bf16).reshape(16, 32, width)

    perm = perm_ref[...]
    grad = permute(dot_nn, perm, g_ref[...])
    mlp_grad = grad.astype(bf16)
    downbg_ref[...] = jnp.sum(mlp_grad.astype(f32), axis=0, keepdims=True)
    hat, inverse = normalise(mid_ref[...])
    normed = (hat * gain_ref[1:2, :] + off_ref[1:2, :]).astype(bf16)
    norm_grad = jnp.zeros((ROWS, WIDTH), f32)
    for m in range(2):
        act_grad = dot_nn(mlp_grad, weight(w_ref, m, QKV + HALF + HID, HID))
        pre_grad = (act_grad * slope_ref[m]).astype(bf16)
        upbg_ref[m : m + 1, :] = jnp.sum(pre_grad.astype(f32), axis=0, keepdims=True)
        put(m, QKV + HALF + HID, HID, dot_tn(mlp_grad, act_ref[m]))
        put(m, QKV + HALF, HID, dot_tn(normed, pre_grad))
        norm_grad = norm_grad + dot_nt(pre_grad, weight(w_ref, m, QKV + HALF, HID))
    back, gain_sum, off_sum = norm_back(norm_grad, hat, inverse, gain_ref[1:2, :])
    gaing_ref[1:2, :] = gain_sum
    offg_ref[1:2, :] = off_sum
    grad = grad + back
    attn_grad = grad.astype(bf16)
    projbg_ref[...] = jnp.sum(attn_grad.astype(f32), axis=0, keepdims=True)
    for m in range(2):
        put(m, QKV, HALF, dot_tn(attn_grad, mixed_ref[m]))
        dmix_ref[m] = dot_nn(attn_grad, weight(w_ref, m, QKV, HALF)).astype(bf16)

    def group(i, carry):
        m = i // 2
        lanes = pl.multiple_of((i % 2) * 128, 128)
        for h in range(4):
            relg_ref[i * 4 + h] = jnp.zeros((128, 128), f32)
        for p in range(2):
            rows = slice(p * 128, p * 128 + 128)
            query = qkv_ref[m, rows, pl.ds(lanes, 128)]
            key = qkv_ref[m, rows, pl.ds(lanes + HALF, 128)]
            value = qkv_ref[m, rows, pl.ds(lanes + 2 * HALF, 128)]
            dmix = dmix_ref[m, rows, pl.ds(lanes, 128)]
            dquery = jnp.zeros((128, 128), f32)
            dkey = jnp.zeros((128, 128), f32)
            dvalue = jnp.zeros((128, 128), f32)
            for h in range(4):
                sel = lane_mask(h)
                query_h = query * sel
                dmix_h = dmix * sel
                probs = head_probs(query_h, key, rel_ref[i * 4 + h], mask_ref[p])
                dvalue = dvalue + dot_tn(probs.astype(bf16), dmix_h)
                dprobs = dot_nt(dmix_h, value)
                dscore = (
                    probs * (dprobs - jnp.sum(probs * dprobs, axis=-1, keepdims=True))
                ).astype(bf16)
                relg_ref[i * 4 + h] += dscore.astype(f32)
                dquery = dquery + dot_nn(dscore, key * sel)
                dkey = dkey + dot_tn(dscore, query_h)
            dqkv_ref[m, rows, pl.ds(lanes, 128)] = (dquery * scaling).astype(bf16)
            dqkv_ref[m, rows, pl.ds(lanes + HALF, 128)] = (dkey * scaling).astype(bf16)
            dqkv_ref[m, rows, pl.ds(lanes + 2 * HALF, 128)] = dvalue.astype(bf16)
        return carry

    lax.fori_loop(0, 4, group, 0)
    hat, inverse = normalise(xw_ref[...])
    normed = (hat * gain_ref[0:1, :] + off_ref[0:1, :]).astype(bf16)
    norm_grad = jnp.zeros((ROWS, WIDTH), f32)
    for m in range(2):
        dqkv = dqkv_ref[m]
        qkvbg_ref[m : m + 1, :] = jnp.sum(dqkv.astype(f32), axis=0, keepdims=True)
        put(m, 0, QKV, dot_tn(normed, dqkv))
        norm_grad = norm_grad + dot_nt(dqkv, weight(w_ref, m, 0, QKV))
    back, gain_sum, off_sum = norm_back(norm_grad, hat, inverse, gain_ref[0:1, :])
    gaing_ref[0:1, :] = gain_sum
    offg_ref[0:1, :] = off_sum
    out_ref[...] = permute(dot_tn, perm, grad + back)


def whole(shape):
    return pl.BlockSpec(shape, lambda i: (0,) * len(shape), pipeline_mode=pl.Buffered(1))


def call_kernel(body, depth, operands, outs, scratch, flops):
    specs = [
        pl.BlockSpec(
            (16, 2, 32, COLS), lambda i: (0, 0, 0, depth), pipeline_mode=pl.Buffered(1)
        )
        if position == 2
        else whole(member.shape)
        for position, member in enumerate(operands)
    ]
    return pl.pallas_call(
        body,
        grid=(1,),
        out_shape=[jax.ShapeDtypeStruct(shape, kind) for shape, kind in outs],
        in_specs=specs,
        out_specs=[whole(shape) for shape, _ in outs],
        scratch_shapes=scratch,
        compiler_params=pltpu.CompilerParams(vmem_limit_bytes=56 * 1024 * 1024),
        cost_estimate=pl.CostEstimate(
            flops=flops, bytes_accessed=20_000_000, transcendentals=2_000_000
        ),
    )(*operands)


def pair_masks(region, roll_by):
    places = token_places(roll_by)
    valid = places >= 0
    labels = region.reshape(-1)[jnp.asarray(np.where(valid, places, 0))]
    if roll_by:
        band = np.zeros((ROWS,), np.int32)
        for window in range(4):
            for at in range(AREA):
                row = (window // 2) * WINDOW + at // WINDOW
                col = (window % 2) * WINDOW + at % WINDOW
                ids = [int(v >= GRID - WINDOW) + int(v >= GRID - roll_by) for v in (row, col)]
                band[window * SLOT + at] = 3 * ids[0] + ids[1]
        labels = labels * 9 + jnp.asarray(band)
    labels = labels.reshape(2, 128)
    window_of = (np.arange(ROWS) // SLOT).reshape(2, 128)
    usable = (window_of[:, :, None] == window_of[:, None, :]) & valid.reshape(2, 1, 128)
    same = labels[:, :, None] == labels[:, None, :]
    return jnp.where(jnp.asarray(usable), jnp.where(same, 0.0, masked_score), blocked).astype(f32)


def pair_index():
    places = np.arange(SLOT)
    row_of, col_of = places // WINDOW, places % WINDOW
    index = (row_of[:, None] - row_of[None, :] + WINDOW - 1) * (2 * WINDOW - 1) + (
        col_of[:, None] - col_of[None, :] + WINDOW - 1
    )
    inside = (places[:, None] < AREA) & (places[None, :] < AREA)
    return np.where(inside, index, -1)


def per_device(
    tokens,
    region_ids,
    norm_gains,
    norm_biases,
    qkv_weight,
    qv_bias,
    rel_table,
    proj_weight,
    proj_bias,
    fc1_weight,
    fc1_bias,
    fc2_weight,
    fc2_bias,
    out_grad,
):
    layer_total = qkv_weight.shape[0]
    n_dp = lax.axis_size("dp")
    devices = n_dp * 2
    both = ("dp", "mp")
    mp_index = lax.axis_index("mp")
    shard_rows = qkv_weight.shape[1]
    count = tokens.shape[0]

    parts = []
    for depth in range(layer_total):
        parts += [
            qkv_weight[depth].reshape(shard_rows, QKV),
            proj_weight[depth].T,
            fc1_weight[depth],
            fc2_weight[depth].T,
        ]
    shard = jnp.concatenate(parts, axis=1)
    weights = lax.all_gather(shard, both, axis=0, tiled=True)
    weights = weights.reshape(n_dp, 2, shard_rows, layer_total * COLS)
    if n_dp != 16:
        weights = weights.transpose(1, 0, 2, 3).reshape(2, 16, 32, layer_total * COLS)
        weights = weights.transpose(1, 0, 2, 3)

    small = jnp.concatenate([qv_bias.reshape(-1), rel_table.reshape(-1), fc1_bias.reshape(-1)])
    other = lax.ppermute(small, "mp", [(0, 1), (1, 0)])
    lower = mp_index == 0
    small = jnp.stack([jnp.where(lower, small, other), jnp.where(lower, other, small)])
    first, second = qv_bias.size, qv_bias.size + rel_table.size
    qv_all = small[:, :first].reshape(2, layer_total, 2, HALF)
    rel_all = small[:, first:second].reshape(2, layer_total, REL, HEADS // 2)
    up_all = small[:, second:].reshape(2, layer_total, HID)

    index = pair_index().reshape(-1)
    hot = jnp.asarray((index[:, None] == np.arange(REL)[None, :]).astype(np.float32)).astype(bf16)
    table = rel_all.transpose(1, 0, 3, 2).reshape(layer_total * HEADS, REL)

    def exact_dot(left, right, dims):
        high = left.astype(bf16)
        rest = left - high.astype(f32)
        mid = rest.astype(bf16)
        low = (rest - mid.astype(f32)).astype(bf16)
        stacked = jnp.concatenate([high, mid, low], axis=0)
        product = lax.dot_general(stacked, right, dims, preferred_element_type=f32)
        product = product.reshape((3,) + (left.shape[0],) + product.shape[1:])
        return (product[0] + product[1]) + product[2]

    relative = exact_dot(table, hot, (((1,), (1,)), ((), ())))
    relative = relative.reshape(layer_total, HEADS, SLOT, SLOT)
    relative = jnp.concatenate([relative, relative], axis=3)

    region = lax.dynamic_index_in_dim(region_ids, mp_index, 0, keepdims=False)
    rolls = [SHIFT if depth % 2 == 1 else 0 for depth in range(layer_total)]
    perms = {roll: jnp.asarray(permutation(roll)).astype(bf16) for roll in (0, SHIFT)}
    masks = {roll: pair_masks(region, roll) for roll in (0, SHIFT)}

    state = jnp.pad(tokens.astype(f32), ((0, ROWS - count), (0, 0)))
    records = []
    for depth in range(layer_total):
        roll = rolls[depth]
        bias = jnp.concatenate(
            [qv_all[:, depth, 0], jnp.zeros((2, HALF), f32), qv_all[:, depth, 1]], axis=1
        )
        operands = (
            state, perms[roll], weights, norm_gains[depth], norm_biases[depth], bias,
            relative[depth], masks[roll], proj_bias[depth][None], up_all[:, depth],
            fc2_bias[depth][None],
        )
        outs = (
            ((ROWS, WIDTH), f32), ((ROWS, WIDTH), f32), ((ROWS, WIDTH), f32),
            ((2, ROWS, QKV), bf16), ((2, ROWS, HALF), bf16),
            ((2, ROWS, HID), f32), ((2, ROWS, HID), bf16),
        )
        state, *saved = call_kernel(forward_kernel, depth, operands, outs, [], 2_000_000_000)
        records.append(saved)
    block_out = state[:count].astype(bf16)

    gradient = jnp.pad(out_grad.astype(f32), ((0, ROWS - count), (0, 0)))
    totals = [None] * layer_total
    small_rows = [None] * layer_total
    for depth in reversed(range(layer_total)):
        roll = rolls[depth]
        operands = (
            gradient, perms[roll], weights, norm_gains[depth], norm_biases[depth],
            relative[depth], masks[roll], *records[depth],
        )
        outs = (
            ((ROWS, WIDTH), f32), ((16, 2, 32, COLS), bf16), ((2, WIDTH), f32), ((2, WIDTH), f32),
            ((2, QKV), f32), ((1, WIDTH), f32), ((2, HID), f32), ((1, WIDTH), f32),
            ((HEADS, 128, 128), f32),
        )
        scratch = [pltpu.VMEM((2, ROWS, HALF), bf16), pltpu.VMEM((2, ROWS, QKV), bf16)]
        gradient, wide, *rest = call_kernel(
            backward_kernel, depth, operands, outs, scratch, 4_000_000_000
        )
        if n_dp != 16:
            wide = wide.transpose(1, 0, 2, 3).reshape(2, n_dp, shard_rows, COLS)
            wide = wide.transpose(1, 0, 2, 3)
        wide = wide.reshape(devices * shard_rows, COLS)
        owned = lax.psum_scatter(wide, both, scatter_dimension=0, tiled=True)
        totals[depth] = owned.astype(f32)
        gain_sum, off_sum, qkvb_sum, projb_sum, upb_sum, downb_sum, rel_sum = rest
        pairs = rel_sum[:, :SLOT, :SLOT] + rel_sum[:, SLOT:, SLOT:]
        qv_sum = jnp.stack([qkvb_sum[:, :HALF], qkvb_sum[:, 2 * HALF :]]).reshape(-1)
        small_rows[depth] = (gain_sum, off_sum, qv_sum, projb_sum, upb_sum, downb_sum, pairs)

    pairs = jnp.concatenate([row[6].reshape(HEADS, -1) for row in small_rows], axis=0)
    table_sum = exact_dot(pairs, hot, (((1,), (0,)), ((), ())))
    member = jnp.concatenate(
        [jnp.concatenate([piece.reshape(-1) for piece in row[:6]]) for row in small_rows]
        + [table_sum.reshape(-1)]
    )
    extent = member.size
    padded = -(-extent // (devices * 128)) * devices * 128
    member = jnp.pad(member, (0, padded - extent)).reshape(devices, padded // devices)
    own = jnp.sum(lax.all_to_all(member, both, 0, 0), axis=0)
    summed = lax.all_gather(own, both, axis=0, tiled=True)
    each = (extent - table_sum.size) // layer_total
    rows = summed[: each * layer_total].reshape(layer_total, each)
    sizes = (2 * WIDTH, 2 * WIDTH, 4 * HALF, WIDTH, 2 * HID, WIDTH)
    edges = np.concatenate([[0], np.cumsum(sizes)])
    gain_t, off_t, qv_t, projb_t, upb_t, downb_t = [
        rows[:, edges[k] : edges[k + 1]] for k in range(6)
    ]
    table_t = summed[each * layer_total : extent].reshape(layer_total, 2, HEADS // 2, REL)
    pick = lambda array, axis: lax.dynamic_index_in_dim(array, mp_index, axis, keepdims=False)
    stacked = jnp.stack(totals)
    ends = np.concatenate([[0], np.cumsum((QKV, HALF, HID, HID))])
    qkv_t, proj_t, up_t, down_t = [stacked[:, :, ends[k] : ends[k + 1]] for k in range(4)]
    return (
        block_out,
        gradient[:count].astype(bf16),
        gain_t.reshape(layer_total, 2, WIDTH),
        off_t.reshape(layer_total, 2, WIDTH),
        qkv_t.reshape(layer_total, shard_rows, 3, HALF),
        pick(qv_t.reshape(layer_total, 2, 2, HALF), 2),
        pick(table_t, 1).transpose(0, 2, 1),
        proj_t.transpose(0, 2, 1),
        projb_t,
        up_t,
        pick(upb_t.reshape(layer_total, 2, HID), 1),
        down_t.transpose(0, 2, 1),
        downb_t,
    )


def solution(mesh):
    in_specs = (
        P(("dp", "mp"), None),
        P("dp", None, None),
        P(),
        P(),
        P(None, "dp", None, "mp"),
        P(None, None, "mp"),
        P(None, None, "mp"),
        P(None, "mp", "dp"),
        P(),
        P(None, "dp", "mp"),
        P(None, "mp"),
        P(None, "mp", "dp"),
        P(),
        P(("dp", "mp"), None),
    )
    out_specs = (
        P(("dp", "mp"), None),
        P(("dp", "mp"), None),
        P(),
        P(),
        P(None, "dp", None, "mp"),
        P(None, None, "mp"),
        P(None, None, "mp"),
        P(None, "mp", "dp"),
        P(),
        P(None, "dp", "mp"),
        P(None, "mp"),
        P(None, "mp", "dp"),
        P(),
    )
    return jax.shard_map(
        per_device, mesh=mesh, in_specs=in_specs, out_specs=out_specs, check_vma=False
    )
```

time: 1140 us -> 431 us (0.38); the launches traced: 1120 us -> 430 us
  waiting for transfers between devices: 590 us -> 231 us
  blocking collectives: 213 us -> 65.5 us
  local copies, waits for them, and re-layouts: 156 us -> 27 us
  matrix products: 78.3 us -> 1.59 us
  Pallas kernels: 0 us -> 72.8 us
  other arithmetic: 44.2 us -> 11.1 us
  starting transfers between devices: 26.9 us -> 5.93 us
    reduce_scatter x8 -> x2, waiting for transfers between devices: 493 us -> 147 us  [per_device(): owned = lax.psum_scatter(wide, both, scatter_dimension=0, tiled=True)]
    psum x1 -> x0, waiting for transfers between devices: 92.8 us -> none  [per_device(): lax.psum((stack_member(0), stack_member(1), qv_full, table_full, stack_me...]
    all_gather x4 -> x1, waiting for transfers between devices: 0.02 us -> 79.2 us  [per_device(): weights = lax.all_gather(shard, both, axis=0, tiled=True)]
    all_gather x12 -> x1, blocking collectives: 143 us -> 65.5 us  [per_device(): summed = lax.all_gather(own, both, axis=0, tiled=True)]
    dot_general x40 -> x2, matrix products: 78.3 us -> 1.59 us  [exact_dot(): product = lax.dot_general(stacked, right, dims, preferred_element_type=f32)]
    pallas_call x0 -> x4, Pallas kernels: none -> 72.8 us  [call_kernel(): pl.pallas_call(body, grid=(1,), out_shape=[jax.ShapeDtypeStruct(shape, ki...]
    unnamed x7 -> x0, blocking collectives: 69.5 us -> none
    unnamed x233 -> x84, local copies, waits for them, and re-layouts: 58.6 us -> 8.45 us
  transfers between devices with their start and end apart: 21 -> 5, of which waited for: 12 -> 4; matrix products, arithmetic and copies ran while one was open for 16% -> 7% of each run, Pallas kernels for 0% -> 0%
where the time goes in v1:
time: 431 us; the launch traced here: 430 us
  waiting for transfers between devices  231 us (54%)
  Pallas kernels  72.8 us (17%)
  blocking collectives  65.5 us (15%)
  local copies, waits for them, and re-layouts  27 us (6%)
  between operations  14.6 us (3%)
  other arithmetic  11.1 us (3%)
  starting transfers between devices  5.93 us (1%)
    reduce_scatter x2, waiting for transfers between devices, per_device(): owned = lax.psum_scatter(wide, both, scatter_dimension=0, tiled=True)  147 us
    all_gather x1, waiting for transfers between devices, per_device(): weights = lax.all_gather(shard, both, axis=0, tiled=True)  79.2 us
    pallas_call x4, Pallas kernels, call_kernel(): pl.pallas_call(body, grid=(1,), out_shape=[jax.ShapeDtypeStruct(shape, ki...  72.8 us
    all_gather x1, blocking collectives, per_device(): summed = lax.all_gather(own, both, axis=0, tiled=True)  65.5 us
  transfers between devices with their start and end apart: 5, of which 4 were waited for; matrix products, arithmetic and copies ran while one was open for 7% of the time, Pallas kernels for 0%

profile of v1, /device:TPU:0, one launch (start us, length us, event | category | flops | bytes accessed | tf_op | source)
XLA Modules:
  0.0 429.9 jit_solution(9005336684336026965)
XLA Ops:
  7.3 0.8 fusion.15
  9.0 0.8 bitcast_dynamic-update-slice_fusion.3
  9.8 0.8 bitcast_dynamic-update-slice_fusion.1
  11.5 0.8 bitcast_dynamic-update-slice_fusion.2
  12.3 0.9 bitcast_dynamic-update-slice_fusion
  15.4 0.8 copy.57
  16.5 3.0 collective-permute-start
  19.6 1.9 gather_fusion.1
  21.6 1.9 gather_fusion
  23.5 0.9 pad_convert_fusion.1.x_ref
  25.6 0.8 select_select_fusion
  26.5 0.9 pad_convert_fusion.g_ref
  28.6 0.9 slice_add_fusion
  29.5 1.5 add.61
  31.0 1.3 fusion.3
  33.6 79.2 %all-gather.3.cloned.1.call-done = bf16[1024,6144]{1,0:T(8,128)(2,1)} async-done(((bf16[32,6144]{1,0:T(8,128)(2,1)}), bf16[1024,6144]{1,0:T(8,128)(2,1)}) %all-gather.3.cloned.1.call-update) | async-done | bytes 12582928 | tf_op jit(solution)/shard_map/all_gather | solution.py:324
  112.8 12.1 %shard_map.309 = (f32[256,512]{1,0:T(8,128)}, f32[256,512]{1,0:T(8,128)}, f32[256,512]{1,0:T(8,128)}, bf16[2,256,768]{2,1,0:T(8,128)(2,1)}, bf16[2,256,256]{2,1,...) custom-call(f32[256,512]{1,0:T(8,128)} %pad_convert_fusion.1.x_ref, ...), custom_call_target="tpu_custom_call" | custom-call | flops 2000000000 | bytes 20000000 | tf_op jit(solution)/shard_map/pallas_call | solution.py:247
  125.0 12.3 %shard_map.310 = (f32[256,512]{1,0:T(8,128)}, f32[256,512]{1,0:T(8,128)}, f32[256,512]{1,0:T(8,128)}, bf16[2,256,768]{2,1,0:T(8,128)(2,1)}, bf16[2,256,256]{2,1,...) custom-call(f32[256,512]{1,0:T(8,128)} %get-tuple-element.45.x_ref, ...), custom_call_target="tpu_custom_call" | custom-call | flops 2000000000 | bytes 20000000 | tf_op jit(solution)/shard_map/pallas_call | solution.py:247
  137.2 24.1 %shard_map.311 = (f32[256,512]{1,0:T(8,128)}, bf16[16,2,32,3072]{3,2,1,0:T(8,128)(2,1)}, f32[2,512]{1,0:T(2,128)}, f32[2,512]{1,0:T(2,128)}, f32[2,768]{1,0:T(2,...) custom-call(f32[256,512]{1,0:T(8,128)} %pad_convert_fusion.g_ref, ...), custom_call_target="tpu_custom_call" | custom-call | flops 4000000000 | bytes 20000000 | tf_op jit(solution)/shard_map/pallas_call | solution.py:247
  161.3 24.3 %shard_map.312 = (f32[256,512]{1,0:T(8,128)}, bf16[16,2,32,3072]{3,2,1,0:T(8,128)(2,1)}, f32[2,512]{1,0:T(2,128)}, f32[2,512]{1,0:T(2,128)}, f32[2,768]{1,0:T(2,...) custom-call(f32[256,512]{1,0:T(8,128)} %get-tuple-element.53.g_ref, ...), custom_call_target="tpu_custom_call" | custom-call | flops 4000000000 | bytes 20000000 | tf_op jit(solution)/shard_map/pallas_call | solution.py:247
  186.6 1.4 slice_add_fusion.3
  188.2 1.4 slice_add_fusion.2
  192.0 2.8 all-to-all-start
  194.9 1.7 slice.311
  196.6 1.7 slice.310
  198.3 4.4 %all-to-all-done = f32[32,1,640]{2,1,0:T(1,128)S(1)} async-done(((f32[32,1,640]{2,1,0:T(1,128)}), f32[32,1,640]{2,1,0:T(1,128)S(1)}, u32[]{:S(2)}, u32[]{:S(2)}) %all-to-all-start) | async-done | bytes 81952 | tf_op jit(solution)/shard_map/all_to_all | solution.py:421
  202.8 65.5 %all-gather = f32[32,1,640]{2,1,0:T(1,128)S(1)} all-gather(f32[1,1,640]{2,1,0:T(1,128)S(1)} %reshape.206), channel_id=1, replica_groups=mesh['dp'=16,'mp'=2] {'dp','mp'}, dimensions={0}, use_global_device_ids=true | all-gather | bytes 84480 | tf_op jit(solution)/shard_map/all_gather | solution.py:422
  272.2 26.8 %reduce-scatter.3.cloned.1.call-done = bf16[32,3072]{1,0:T(8,128)(2,1)} async-done(((bf16[1024,3072]{1,0:T(8,128)(2,1)}), bf16[32,3072]{1,0:T(8,128)(2,1)}) %reduce-scatter.3.cloned.1.call-update) | async-done | bytes 196624 | tf_op jit(solution)/shard_map/reduce_scatter | solution.py:405
  299.0 120.4 %reduce-scatter.5.cloned.1.call-done = bf16[32,3072]{1,0:T(8,128)(2,1)} async-done(((bf16[1024,3072]{1,0:T(8,128)(2,1)}), bf16[32,3072]{1,0:T(8,128)(2,1)}) %reduce-scatter.5.cloned.1.call-update) | async-done | bytes 196624 | tf_op jit(solution)/shard_map/reduce_scatter | solution.py:405
  419.4 1.4 convert_bitcast_fusion
  420.8 1.1 maximum_convert_fusion
  421.9 0.8 slice_bitcast_fusion
  (144 shorter events, 15.7 us)
Async XLA Ops:
  7.2 12.3 %copy-start = (s32[2,14,14]{2,0,1:T(2,128)S(1)}, s32[2,14,14]{2,0,1:T(2,128)}, u32[]{:S(2)}) copy-start(s32[2,14,14]{2,0,1:T(2,128)} %param.23) | copy-start | bytes 4708
  7.2 12.4 %copy-start.23 = (s32[256]{0:T(256)S(1)}, s32[256]{0:T(256)}, u32[]{:S(2)}) copy-start(s32[256]{0:T(256)} %constant.80) | copy-start | bytes 3076
  7.2 12.4 %copy-start.24 = (s32[256]{0:T(256)S(1)}, s32[256]{0:T(256)}, u32[]{:S(2)}) copy-start(s32[256]{0:T(256)} %constant.79) | copy-start | bytes 3076
  7.2 105.6 %all-gather.3.cloned.1.call-start = ((), (), s32[]{:S(2)}) async-start(), calls=%async_computation.3 | async-start | bytes 12976128 | tf_op jit(solution)/shard_map/all_gather | solution.py:324
  8.1 15.4 %copy-start.3 = (bf16[196,512]{1,0:T(8,128)(2,1)S(1)}, bf16[196,512]{1,0:T(8,128)(2,1)}, u32[]{:S(2)}) copy-start(bf16[196,512]{1,0:T(8,128)(2,1)} %param.22) | copy-start | bytes 602116
  10.7 13.7 %copy-start.22 = (s32[256]{0:T(256)S(1)}, s32[256]{0:T(256)}, u32[]{:S(2)}) copy-start(s32[256]{0:T(256)} %constant.58.clone) | copy-start | bytes 3076
  10.7 13.7 %copy-start.14 = (f32[2,512]{1,0:T(2,128)S(1)}, f32[2,512]{1,0:T(2,128)}, u32[]{:S(2)}) copy-start(f32[2,512]{1,0:T(2,128)} %param.34) | copy-start | bytes 12292
  10.7 13.7 %copy-start.15 = (f32[2,512]{1,0:T(2,128)S(1)}, f32[2,512]{1,0:T(2,128)}, u32[]{:S(2)}) copy-start(f32[2,512]{1,0:T(2,128)} %param.30) | copy-start | bytes 12292
  10.7 14.3 %copy-start.8 = (f32[2,2,512]{2,1,0:T(2,128)S(1)}, f32[2,2,512]{2,1,0:T(2,128)}, u32[]{:S(2)}) copy-start(f32[2,2,512]{2,1,0:T(2,128)} %param.25) | copy-start | bytes 24580
  10.7 14.3 %copy-start.9 = (f32[2,2,512]{2,1,0:T(2,128)S(1)}, f32[2,2,512]{2,1,0:T(2,128)}, u32[]{:S(2)}) copy-start(f32[2,2,512]{2,1,0:T(2,128)} %param.24) | copy-start | bytes 24580
  10.7 14.9 %copy-start.5 = (pred[2,128,128]{2,1,0:T(32,128)(4,1)S(1)}, pred[2,128,128]{2,1,0:T(32,128)(4,1)}, u32[]{:S(2)}) copy-start(pred[2,128,128]{2,1,0:T(32,128)(4,1)} %constant.56.clone) | copy-start | bytes 98308
  12.3 14.1 %copy-start.4 = (bf16[196,512]{1,0:T(8,128)(2,1)S(1)}, bf16[196,512]{1,0:T(8,128)(2,1)}, u32[]{:S(2)}) copy-start(bf16[196,512]{1,0:T(8,128)(2,1)} %param.35) | copy-start | bytes 602116
  13.2 0.8 copy-start.2
  14.0 285.0 %reduce-scatter.3.cloned.1.call-start = ((), (), s32[]{:S(2)}) async-start(), calls=%async_computation.4 | async-start | bytes 6488064 | tf_op jit(solution)/shard_map/reduce_scatter | solution.py:405
  16.5 10.8 %collective-permute-start = (f32[5776]{0:T(1024)S(1)}, f32[5776]{0:T(1024)S(1)}, u32[]{:S(2)}, u32[]{:S(2)}) collective-permute-start(f32[5776]{0:T(1024)S(1)} %concatenate.28), channel_id=1, source_target_pairs={{0,1},{1,0},{2,3},{3,2},{4,5},{5,4},{6,7},{7,6},{8,9},{9,8},{10,11... | collective-permute-start | bytes 69320 | tf_op jit(solution)/shard_map/ppermute | solution.py:331
  21.6 6.3 %copy-start.1 = (bf16[4096,169]{1,0:T(8,128)(2,1)S(1)}, bf16[4096,169]{1,0:T(8,128)(2,1)}, u32[]{:S(2)}) copy-start(bf16[4096,169]{1,0:T(8,128)(2,1)} %constant.69) | copy-start | bytes 4153348
  185.7 233.7 %reduce-scatter.5.cloned.1.call-start = ((), (), s32[]{:S(2)}) async-start(), calls=%async_computation.5 | async-start | bytes 6488064 | tf_op jit(solution)/shard_map/reduce_scatter | solution.py:405
  185.7 0.7 copy-start.13
  185.7 0.7 copy-start.11
  185.7 0.7 copy-start.12
  185.8 0.7 copy-start.10
  185.8 0.7 copy-start.17
  185.8 0.8 copy-start.16
  189.9 1.3 copy-start.21
  189.9 1.3 copy-start.7
  189.9 1.3 copy-start.20
  190.0 1.3 copy-start.19
  190.0 1.4 copy-start.6
  190.0 1.4 copy-start.18
  192.0 10.7 %all-to-all-start = ((f32[32,1,640]{2,1,0:T(1,128)}), f32[32,1,640]{2,1,0:T(1,128)S(1)}, u32[]{:S(2)}, u32[]{:S(2)}) async-start(f32[32,1,640]{2,1,0:T(1,128)} %bitcast.37), calls=%async_computation | async-start | bytes 163840 | tf_op jit(solution)/shard_map/all_to_all | solution.py:421
Sparse Core Ops, SparseCore 0:
  14.1 98.6 all-gather.2
  185.8 113.1 reduce-scatter.2
  305.6 113.7 reduce-scatter.4

commit v2 on v1

--- a/solution.py
+++ b/solution.py
@@ -235,7 +235,7 @@
     return pl.BlockSpec(shape, lambda i: (0,) * len(shape), pipeline_mode=pl.Buffered(1))
 
 
-def call_kernel(body, depth, operands, outs, scratch, flops):
+def call_kernel(body, depth, operands, outs, scratch, flops, wide_at=None, shared=None):
     specs = [
         pl.BlockSpec(
             (16, 2, 32, COLS), lambda i: (0, 0, 0, depth), pipeline_mode=pl.Buffered(1)
@@ -244,12 +244,25 @@
         else whole(member.shape)
         for position, member in enumerate(operands)
     ]
+    out_specs = [whole(shape) for shape, _ in outs]
+    aliases = {}
+    if wide_at is not None:
+        out_specs[wide_at] = pl.BlockSpec(
+            (16, 2, 32, COLS), lambda i: (0, 0, 0, depth), pipeline_mode=pl.Buffered(1)
+        )
+    if shared is not None:
+        aliases = {len(operands): wide_at}
+        operands = tuple(operands) + (shared,)
+        specs.append(pl.BlockSpec(memory_space=pl.ANY))
+        plain, taken = body, len(operands) - 1
+        body = lambda *refs: plain(*refs[:taken], *refs[taken + 1 :])
     return pl.pallas_call(
         body,
         grid=(1,),
         out_shape=[jax.ShapeDtypeStruct(shape, kind) for shape, kind in outs],
         in_specs=specs,
-        out_specs=[whole(shape) for shape, _ in outs],
+        out_specs=out_specs,
+        input_output_aliases=aliases,
         scratch_shapes=scratch,
         compiler_params=pltpu.CompilerParams(vmem_limit_bytes=56 * 1024 * 1024),
         cost_estimate=pl.CostEstimate(
@@ -381,7 +394,7 @@
     block_out = state[:count].astype(bf16)
 
     gradient = jnp.pad(out_grad.astype(f32), ((0, ROWS - count), (0, 0)))
-    totals = [None] * layer_total
+    wide = None
     small_rows = [None] * layer_total
     for depth in reversed(range(layer_total)):
         roll = rolls[depth]
@@ -390,24 +403,24 @@
             relative[depth], masks[roll], *records[depth],
         )
         outs = (
-            ((ROWS, WIDTH), f32), ((16, 2, 32, COLS), bf16), ((2, WIDTH), f32), ((2, WIDTH), f32),
+            ((ROWS, WIDTH), f32), ((16, 2, 32, layer_total * COLS), bf16), ((2, WIDTH), f32), ((2, WIDTH), f32),
             ((2, QKV), f32), ((1, WIDTH), f32), ((2, HID), f32), ((1, WIDTH), f32),
             ((HEADS, 128, 128), f32),
         )
         scratch = [pltpu.VMEM((2, ROWS, HALF), bf16), pltpu.VMEM((2, ROWS, QKV), bf16)]
         gradient, wide, *rest = call_kernel(
-            backward_kernel, depth, operands, outs, scratch, 4_000_000_000
-        )
-        if n_dp != 16:
-            wide = wide.transpose(1, 0, 2, 3).reshape(2, n_dp, shard_rows, COLS)
-            wide = wide.transpose(1, 0, 2, 3)
-        wide = wide.reshape(devices * shard_rows, COLS)
-        owned = lax.psum_scatter(wide, both, scatter_dimension=0, tiled=True)
-        totals[depth] = owned.astype(f32)
+            backward_kernel, depth, operands, outs, scratch, 4_000_000_000, 1, wide
+        )
         gain_sum, off_sum, qkvb_sum, projb_sum, upb_sum, downb_sum, rel_sum = rest
         pairs = rel_sum[:, :SLOT, :SLOT] + rel_sum[:, SLOT:, SLOT:]
         qv_sum = jnp.stack([qkvb_sum[:, :HALF], qkvb_sum[:, 2 * HALF :]]).reshape(-1)
         small_rows[depth] = (gain_sum, off_sum, qv_sum, projb_sum, upb_sum, downb_sum, pairs)
+
+    if n_dp != 16:
+        wide = wide.transpose(1, 0, 2, 3).reshape(2, n_dp, shard_rows, layer_total * COLS)
+        wide = wide.transpose(1, 0, 2, 3)
+    wide = wide.reshape(devices * shard_rows, layer_total * COLS)
+    owned = lax.psum_scatter(wide, both, scatter_dimension=0, tiled=True).astype(f32)
 
     pairs = jnp.concatenate([row[6].reshape(HEADS, -1) for row in small_rows], axis=0)
     table_sum = exact_dot(pairs, hot, (((1,), (0,)), ((), ())))
@@ -429,7 +442,7 @@
     ]
     table_t = summed[each * layer_total : extent].reshape(layer_total, 2, HEADS // 2, REL)
     pick = lambda array, axis: lax.dynamic_index_in_dim(array, mp_index, axis, keepdims=False)
-    stacked = jnp.stack(totals)
+    stacked = owned.reshape(shard_rows, layer_total, COLS).transpose(1, 0, 2)
     ends = np.concatenate([[0], np.cumsum((QKV, HALF, HID, HID))])
     qkv_t, proj_t, up_t, down_t = [stacked[:, :, ends[k] : ends[k + 1]] for k in range(4)]
     return (

time: 431 us -> 352 us (0.82)
  waiting for transfers between devices: 231 us -> 150 us
    reduce_scatter x2 -> x1, waiting for transfers between devices: 147 us -> 66.8 us  [per_device(): lax.psum_scatter(wide, both, scatter_dimension=0, tiled=True).astype(f32)]
    unnamed x84 -> x88, local copies, waits for them, and re-layouts: 8.45 us -> 12 us
  transfers between devices with their start and end apart: 5 -> 4, of which waited for: 4 -> 3; matrix products, arithmetic and copies ran while one was open for 7% -> 8% of each run, Pallas kernels for 0% -> 0%
where the time goes in v2:
time: 352 us; the launch traced here: 351 us
  waiting for transfers between devices  150 us (43%)
  Pallas kernels  72.7 us (21%)
  blocking collectives  66.2 us (19%)
  local copies, waits for them, and re-layouts  31.1 us (9%)
  between operations  14.8 us (4%)
  other arithmetic  8.67 us (2%)
  starting transfers between devices  5.89 us (2%)
    all_gather x1, waiting for transfers between devices, per_device(): weights = lax.all_gather(shard, both, axis=0, tiled=True)  79.2 us
    pallas_call x4, Pallas kernels, call_kernel(): pl.pallas_call(body, grid=(1,), out_shape=[jax.ShapeDtypeStruct(shape, ki...  72.7 us
    reduce_scatter x1, waiting for transfers between devices, per_device(): lax.psum_scatter(wide, both, scatter_dimension=0, tiled=True).astype(f32)  66.8 us
    all_gather x1, blocking collectives, per_device(): summed = lax.all_gather(own, both, axis=0, tiled=True)  66.2 us
    unnamed x88, local copies, waits for them, and re-layouts  12 us
  transfers between devices with their start and end apart: 4, of which 3 were waited for; matrix products, arithmetic and copies ran while one was open for 8% of the time, Pallas kernels for 0%

profile of v2, /device:TPU:0, one launch (start us, length us, event | category | flops | bytes accessed | tf_op | source)
XLA Modules:
  0.0 351.3 jit_solution(8724868329592022638)
XLA Ops:
  7.3 0.8 fusion.15
  9.0 0.8 bitcast_dynamic-update-slice_fusion.3
  9.8 0.8 bitcast_dynamic-update-slice_fusion.1
  11.5 0.8 bitcast_dynamic-update-slice_fusion.2
  12.3 0.9 bitcast_dynamic-update-slice_fusion
  15.4 0.8 copy.70
  16.5 3.0 collective-permute-start
  19.6 1.9 gather_fusion.1
  21.6 1.9 gather_fusion
  23.5 0.8 pad_convert_fusion.1.x_ref
  25.6 0.8 select_select_fusion
  26.4 0.9 pad_convert_fusion.g_ref
  28.6 0.9 slice_add_fusion
  29.5 1.5 add.59
  31.0 1.4 fusion.3
  33.6 79.2 %all-gather.3.cloned.1.call-done = bf16[1024,6144]{1,0:T(8,128)(2,1)} async-done(((bf16[32,6144]{1,0:T(8,128)(2,1)}), bf16[1024,6144]{1,0:T(8,128)(2,1)}) %all-gather.3.cloned.1.call-update) | async-done | bytes 12582928 | tf_op jit(solution)/shard_map/all_gather | solution.py:337
  112.8 12.1 %shard_map.309 = (f32[256,512]{1,0:T(8,128)}, f32[256,512]{1,0:T(8,128)}, f32[256,512]{1,0:T(8,128)}, bf16[2,256,768]{2,1,0:T(8,128)(2,1)}, bf16[2,256,256]{2,1,...) custom-call(f32[256,512]{1,0:T(8,128)} %pad_convert_fusion.1.x_ref, ...), custom_call_target="tpu_custom_call" | custom-call | flops 2000000000 | bytes 20000000 | tf_op jit(solution)/shard_map/pallas_call | solution.py:259
  124.9 12.2 %shard_map.310 = (f32[256,512]{1,0:T(8,128)}, f32[256,512]{1,0:T(8,128)}, f32[256,512]{1,0:T(8,128)}, bf16[2,256,768]{2,1,0:T(8,128)(2,1)}, bf16[2,256,256]{2,1,...) custom-call(f32[256,512]{1,0:T(8,128)} %get-tuple-element.45.x_ref, ...), custom_call_target="tpu_custom_call" | custom-call | flops 2000000000 | bytes 20000000 | tf_op jit(solution)/shard_map/pallas_call | solution.py:259
  137.2 24.1 %shard_map.311 = (f32[256,512]{1,0:T(8,128)}, bf16[16,2,32,6144]{3,2,1,0:T(8,128)(2,1)}, f32[2,512]{1,0:T(2,128)}, f32[2,512]{1,0:T(2,128)}, f32[2,768]{1,0:T(2,...) custom-call(f32[256,512]{1,0:T(8,128)} %pad_convert_fusion.g_ref, ...), custom_call_target="tpu_custom_call" | custom-call | flops 4000000000 | bytes 20000000 | tf_op jit(solution)/shard_map/pallas_call | solution.py:259
  161.2 24.3 %shard_map.312 = (f32[256,512]{1,0:T(8,128)}, bf16[16,2,32,6144]{3,2,1,0:T(8,128)(2,1)}, f32[2,512]{1,0:T(2,128)}, f32[2,512]{1,0:T(2,128)}, f32[2,768]{1,0:T(2,...) custom-call(f32[256,512]{1,0:T(8,128)} %get-tuple-element.53.refs_0_, ...), custom_call_target="tpu_custom_call", output_to_operand_aliasing={{1}: (13, {})} | custom-call | flops 4000000000 | bytes 20000000 | tf_op jit(solution)/shard_map/pallas_call | solution.py:259
  186.4 1.4 slice_add_fusion.3
  188.0 1.4 slice_add_fusion.2
  189.8 0.8 fusion
  191.8 2.8 all-to-all-start
  194.7 1.8 slice.313
  196.4 1.7 slice.312
  198.1 4.4 %all-to-all-done = f32[32,1,640]{2,1,0:T(1,128)S(1)} async-done(((f32[32,1,640]{2,1,0:T(1,128)}), f32[32,1,640]{2,1,0:T(1,128)S(1)}, u32[]{:S(2)}, u32[]{:S(2)}) %all-to-all-start) | async-done | bytes 81952 | tf_op jit(solution)/shard_map/all_to_all | solution.py:434
  202.6 66.2 %all-gather = f32[32,1,640]{2,1,0:T(1,128)S(1)} all-gather(f32[1,1,640]{2,1,0:T(1,128)S(1)} %reshape.208), channel_id=1, replica_groups=mesh['dp'=16,'mp'=2] {'dp','mp'}, dimensions={0}, use_global_device_ids=true | all-gather | bytes 84480 | tf_op jit(solution)/shard_map/all_gather | solution.py:435
  272.7 66.8 %reduce-scatter.2.cloned.1.call-done = bf16[32,6144]{1,0:T(8,128)(2,1)} async-done(((bf16[1024,6144]{1,0:T(8,128)(2,1)}), bf16[32,6144]{1,0:T(8,128)(2,1)}) %reduce-scatter.2.cloned.1.call-update) | async-done | bytes 393232 | tf_op jit(solution)/shard_map/reduce_scatter | solution.py:423
  339.5 1.8 reshape.191
  342.0 0.8 copy.78
  343.7 0.8 copy.77
  (145 shorter events, 15.8 us)
Async XLA Ops:
  7.2 12.3 %copy-start = (s32[2,14,14]{2,0,1:T(2,128)S(1)}, s32[2,14,14]{2,0,1:T(2,128)}, u32[]{:S(2)}) copy-start(s32[2,14,14]{2,0,1:T(2,128)} %param.23) | copy-start | bytes 4708
  7.2 12.4 %copy-start.23 = (s32[256]{0:T(256)S(1)}, s32[256]{0:T(256)}, u32[]{:S(2)}) copy-start(s32[256]{0:T(256)} %constant.80) | copy-start | bytes 3076
  7.2 12.4 %copy-start.24 = (s32[256]{0:T(256)S(1)}, s32[256]{0:T(256)}, u32[]{:S(2)}) copy-start(s32[256]{0:T(256)} %constant.79) | copy-start | bytes 3076
  7.2 105.6 %all-gather.3.cloned.1.call-start = ((), (), s32[]{:S(2)}) async-start(), calls=%async_computation.2 | async-start | bytes 12976128 | tf_op jit(solution)/shard_map/all_gather | solution.py:337
  8.1 15.4 %copy-start.3 = (bf16[196,512]{1,0:T(8,128)(2,1)S(1)}, bf16[196,512]{1,0:T(8,128)(2,1)}, u32[]{:S(2)}) copy-start(bf16[196,512]{1,0:T(8,128)(2,1)} %param.22) | copy-start | bytes 602116
  10.7 13.7 %copy-start.22 = (s32[256]{0:T(256)S(1)}, s32[256]{0:T(256)}, u32[]{:S(2)}) copy-start(s32[256]{0:T(256)} %constant.58.clone) | copy-start | bytes 3076
  10.7 13.7 %copy-start.14 = (f32[2,512]{1,0:T(2,128)S(1)}, f32[2,512]{1,0:T(2,128)}, u32[]{:S(2)}) copy-start(f32[2,512]{1,0:T(2,128)} %param.34) | copy-start | bytes 12292
  10.7 13.7 %copy-start.15 = (f32[2,512]{1,0:T(2,128)S(1)}, f32[2,512]{1,0:T(2,128)}, u32[]{:S(2)}) copy-start(f32[2,512]{1,0:T(2,128)} %param.30) | copy-start | bytes 12292
  10.7 14.3 %copy-start.8 = (f32[2,2,512]{2,1,0:T(2,128)S(1)}, f32[2,2,512]{2,1,0:T(2,128)}, u32[]{:S(2)}) copy-start(f32[2,2,512]{2,1,0:T(2,128)} %param.25) | copy-start | bytes 24580
  10.7 14.3 %copy-start.9 = (f32[2,2,512]{2,1,0:T(2,128)S(1)}, f32[2,2,512]{2,1,0:T(2,128)}, u32[]{:S(2)}) copy-start(f32[2,2,512]{2,1,0:T(2,128)} %param.24) | copy-start | bytes 24580
  10.7 14.9 %copy-start.5 = (pred[2,128,128]{2,1,0:T(32,128)(4,1)S(1)}, pred[2,128,128]{2,1,0:T(32,128)(4,1)}, u32[]{:S(2)}) copy-start(pred[2,128,128]{2,1,0:T(32,128)(4,1)} %constant.56.clone) | copy-start | bytes 98308
  12.3 14.1 %copy-start.4 = (bf16[196,512]{1,0:T(8,128)(2,1)S(1)}, bf16[196,512]{1,0:T(8,128)(2,1)}, u32[]{:S(2)}) copy-start(bf16[196,512]{1,0:T(8,128)(2,1)} %param.35) | copy-start | bytes 602116
  13.2 0.7 copy-start.2
  14.0 325.5 %reduce-scatter.2.cloned.1.call-start = ((), (), s32[]{:S(2)}) async-start(), calls=%async_computation.3 | async-start | bytes 12976128 | tf_op jit(solution)/shard_map/reduce_scatter | solution.py:423
  16.5 10.8 %collective-permute-start = (f32[5776]{0:T(1024)S(1)}, f32[5776]{0:T(1024)S(1)}, u32[]{:S(2)}, u32[]{:S(2)}) collective-permute-start(f32[5776]{0:T(1024)S(1)} %concatenate.28), channel_id=1, source_target_pairs={{0,1},{1,0},{2,3},{3,2},{4,5},{5,4},{6,7},{7,6},{8,9},{9,8},{10,11... | collective-permute-start | bytes 69320 | tf_op jit(solution)/shard_map/ppermute | solution.py:344
  21.5 6.3 %copy-start.1 = (bf16[4096,169]{1,0:T(8,128)(2,1)S(1)}, bf16[4096,169]{1,0:T(8,128)(2,1)}, u32[]{:S(2)}) copy-start(bf16[4096,169]{1,0:T(8,128)(2,1)} %constant.69) | copy-start | bytes 4153348
  185.6 0.7 copy-start.13
  185.6 0.7 copy-start.12
  185.6 0.7 copy-start.11
  185.6 0.7 copy-start.10
  185.6 0.7 copy-start.17
  185.6 0.7 copy-start.16
  189.7 1.3 copy-start.21
  189.7 1.3 copy-start.7
  189.8 1.3 copy-start.20
  189.8 1.3 copy-start.19
  189.8 1.4 copy-start.6
  189.8 1.4 copy-start.18
  191.8 10.7 %all-to-all-start = ((f32[32,1,640]{2,1,0:T(1,128)}), f32[32,1,640]{2,1,0:T(1,128)S(1)}, u32[]{:S(2)}, u32[]{:S(2)}) async-start(f32[32,1,640]{2,1,0:T(1,128)} %bitcast.37), calls=%async_computation | async-start | bytes 163840 | tf_op jit(solution)/shard_map/all_to_all | solution.py:434
Sparse Core Ops, SparseCore 0:
  14.1 98.6 all-gather.2
  185.8 153.6 reduce-scatter.1
